TPU v7x, 512 devices: a whole 4x8x8 slice. The times are simulated.
512 devices in a mesh: half: 2 (over x_lo), grid: 8 (over y), dom: 32 (over z, x_hi, core).
Axes of the slice: x: 4 (x_hi: 2, x_lo: 2; x = x_hi * 2 + x_lo), y: 8, z: 8, core: 2. Of those that a mesh axis runs over, the one named last changes fastest.
Arguments:
- grids: float32 [16, 64, 64, 4096], P(('half', 'grid'), 'dom'), may hold values from -0.8 to 0.8
- levels: int32 [16, 4], replicated, may hold values from 4 to 6, as said below
Outputs:
- combined: float32 [16, 64, 64, 4096], P(('half', 'grid'), 'dom')
Inputs may be any that keep to these rules, and one draw needn't show every extreme that they name: `levels`: with base b = (4, 5, 5, 5), rows 0 to 7 are b plus, in some order, (2,1,1,0), (2,1,0,1), (2,0,1,1), (1,1,1,1), (1,1,0,0), (1,0,1,0), (1,0,0,1), (0,0,0,0); rows 8 to 15 are b plus, in some order, (2,1,0,0), (2,0,1,0), (2,0,0,1), (1,1,1,0), (1,1,0,1), (1,0,1,1), (2,0,0,0), (1,0,0,0).
All inputs are finite; a program needn't handle non-finite values.
Results may differ from a plain program's by a relative error of at most 0.0003.
Values sent between devices are 32-bit elements; how exact they have to be, the bound alone decides.
A program may use at most 128 MiB of HBM per device.

v0:
```python
import jax
import jax.numpy as jnp
import numpy as np
from jax import lax
from jax.sharding import PartitionSpec as P

LEV1 = 6
LEV2 = 6
LEV3 = 6
LEV4 = 6
N1 = 64
N2 = 64
N3 = 64
N4 = 64
HIGH = lax.Precision.HIGHEST
SPANS = (2, 1, 1, 1)


def level_ordering(level):
    points = 2**level
    ordering = [0]
    for section in range(1, level + 1):
        stride = 2 ** (level - section)
        ordering.extend(range(stride, points, 2 * stride))
    return np.array(ordering)


def hier_tables(level_top, spread):
    size_top = 2**level_top
    forwards = np.zeros((spread + 1, size_top, size_top))
    backwards = np.zeros((spread + 1, size_top, size_top))
    for offset in range(spread + 1):
        level = level_top - spread + offset
        points = 2**level
        down_rows = np.eye(points)
        up_rows = np.eye(points)
        for section in range(level, 0, -1):
            stride = 2 ** (level - section)
            odd_points = np.arange(stride, points, 2 * stride)
            down_rows[odd_points] = down_rows[odd_points] - 0.5 * (
                down_rows[odd_points - stride] + down_rows[(odd_points + stride) % points]
            )
        for section in range(1, level + 1):
            stride = 2 ** (level - section)
            odd_points = np.arange(stride, points, 2 * stride)
            up_rows[odd_points] = up_rows[odd_points] + 0.5 * (
                up_rows[odd_points - stride] + up_rows[(odd_points + stride) % points]
            )
        ordering = level_ordering(level)
        forwards[offset, :points, :points] = down_rows[ordering]
        backwards[offset, :points, :points] = up_rows[:, ordering]
    return (jnp.asarray(forwards, jnp.float32), jnp.asarray(backwards, jnp.float32))


def combination_weights(levels):
    corners = np.array(
        [[corner >> place & 1 for place in range(4)] for corner in range(16)], dtype=np.int32
    )
    parity = 1 - 2 * (corners.sum(axis=1) % 2)
    raised = levels[:, None, :] + jnp.asarray(corners, dtype=jnp.int32)[None, :, :]
    below = jnp.all(raised[:, :, None, :] <= levels[None, None, :, :], axis=3)
    inside = jnp.any(below, axis=2).astype(jnp.int32)
    return jnp.sum(inside * jnp.asarray(parity, dtype=jnp.int32)[None, :], axis=1)


def pick_tables(tables, level_column, level_top, spread):
    shifted = level_column - (level_top - spread)
    onehot = (jnp.arange(spread + 1, dtype=jnp.int32)[None, :] == shifted[:, None]).astype(
        jnp.float32
    )
    return jnp.einsum("gs,sij->gij", onehot, tables, precision=HIGH)


def block_cover(levels, upper_block):
    lowest = jnp.array([LEV1 - 2, LEV2 - 1, LEV3 - 1, LEV4 - 1], dtype=jnp.int32)
    offsets = levels - lowest[None, :]
    blocks = jnp.arange(16, dtype=jnp.int32)
    first_block = jnp.minimum(blocks // 4, 2)
    third_block = blocks // 2 % 2
    fourth_block = blocks % 2
    covered = first_block[None, :] <= offsets[:, 0:1]
    covered = covered & (upper_block <= offsets[:, 1:2])
    covered = covered & (third_block[None, :] <= offsets[:, 2:3])
    return covered & (fourth_block[None, :] <= offsets[:, 3:4])


def compact_order(mask):
    ranking = jnp.argsort(jnp.where(mask, 0, 16) + jnp.arange(16, dtype=jnp.int32))
    return (ranking, mask[ranking].astype(jnp.float32))


def pick_rows(blocks, order, valid):
    return jnp.take(blocks, order, axis=0) * valid[:, None]


def place_rows(rows, order, valid):
    return jnp.zeros((16, rows.shape[1]), jnp.float32).at[order].add(rows * valid[:, None])


def combine(blocks, covered):
    order, valid = compact_order(jnp.any(covered, axis=0))
    summed = lax.psum(pick_rows(blocks, order, valid), ("half", "grid"))
    return place_rows(summed, order, valid)


def per_device(grids, levels):
    finest = (LEV1, LEV2, LEV3, LEV4)
    local_count = grids.shape[0]
    rows_here = grids.shape[1]
    grid_count = lax.axis_size("grid")
    group = lax.axis_index("half") * grid_count + lax.axis_index("grid")
    weights = combination_weights(levels).astype(jnp.float32)
    own_levels = lax.dynamic_slice_in_dim(levels, group * local_count, local_count, 0)
    own_weights = lax.dynamic_slice_in_dim(weights, group * local_count, local_count, 0)
    forward_mats = []
    backward_mats = []
    for axis_index in range(4):
        down_tables, up_tables = hier_tables(finest[axis_index], SPANS[axis_index])
        forward_mats.append(
            pick_tables(
                down_tables, own_levels[:, axis_index], finest[axis_index], SPANS[axis_index]
            )
        )
        backward_mats.append(
            pick_tables(up_tables, own_levels[:, axis_index], finest[axis_index], SPANS[axis_index])
        )
    values = grids.reshape(local_count, rows_here, N2, N3, N4)
    values = jnp.einsum("gjl,gabcl->gabcj", forward_mats[3], values, precision=HIGH)
    values = jnp.einsum("gjc,gabcl->gabjl", forward_mats[2], values, precision=HIGH)
    values = jnp.einsum(
        "gjb,gabm->gajm",
        forward_mats[1],
        values.reshape(local_count, rows_here, N2, N3 * N4),
        precision=HIGH,
    )
    surplus = jnp.einsum(
        "gja,gabm->gjbm",
        forward_mats[0],
        lax.all_to_all(values, "dom", split_axis=2, concat_axis=1, tiled=True),
        precision=HIGH,
    )
    scaled = jnp.einsum("g,gjbm->jbm", own_weights, surplus, precision=HIGH)
    pole_rows = scaled.shape[1]
    upper_block = lax.axis_index("dom") * pole_rows // (N2 // 2)
    covered = block_cover(levels, upper_block)
    quarter_rows = N1 // 4
    blocks = (
        scaled.reshape(4, quarter_rows, pole_rows, 2, N3 // 2, 2, N4 // 2)
        .transpose(0, 3, 5, 1, 2, 4, 6)
        .reshape(16, -1)
    )
    summed_blocks = combine(blocks, covered)
    totals = (
        summed_blocks.reshape(4, 2, 2, quarter_rows, pole_rows, N3 // 2, N4 // 2)
        .transpose(0, 3, 4, 1, 5, 2, 6)
        .reshape(N1, pole_rows, N3 * N4)
    )
    expanded = jnp.einsum("gja,abm->gjbm", backward_mats[0], totals, precision=HIGH)
    returned = lax.all_to_all(expanded, "dom", split_axis=1, concat_axis=2, tiled=True)
    returned = jnp.einsum("gjb,gabm->gajm", backward_mats[1], returned, precision=HIGH)
    returned = returned.reshape(local_count, rows_here, N2, N3, N4)
    returned = jnp.einsum("gjc,gabcl->gabjl", backward_mats[2], returned, precision=HIGH)
    returned = jnp.einsum("gjl,gabcl->gabcj", backward_mats[3], returned, precision=HIGH)
    return returned.reshape(local_count, rows_here, N2, N3 * N4)


def solution(mesh):
    return jax.shard_map(
        per_device,
        mesh=mesh,
        in_specs=(P(("half", "grid"), "dom", None, None), P()),
        out_specs=P(("half", "grid"), "dom", None, None),
        check_vma=False,
    )
```

profile of v0, /device:TPU:1, one launch (start us, length us, event | category | flops | bytes accessed | tf_op | source)
XLA Modules:
  0.0 454.5 jit_solution(10062554610760000204)
XLA Ops:
  6.5 0.8 constant_dynamic-slice_fusion
  7.3 0.6 fusion.27
  7.8 4.6 %reshape.191 = f32[2,64,64,64]{3,2,1,0:T(8,128)} reshape(f32[1,2,64,4096]{3,2,1,0:T(8,128)} %param.13) | data formatting | bytes 4194304 | tf_op jit(solution)/shard_map/reshape.17
  13.7 0.0 copy-done.8
  13.7 0.2 fusion.16
  14.0 0.2 fusion.14
  14.2 13.8 %fusion.28 = f32[64,2,64,64]{3,0,2,1:T(8,128)S(1)} fusion(f32[64,64,1,1]{1,0,3,2:T(8,128)S(1)} %bitcast.162, f32[2,64,64,64]{3,2,1,0:T(8,128)} %reshape.191), kind=kOutput, calls=%fused_computation.65 | convolution fusion | flops 402653184 | bytes 4210688 | tf_op jit(solution)/shard_map/gjl,gabcl->gabcj/dot_general | solution.py:128
  28.0 4.9 %fusion.4 = f32[1,2,64,64,64]{3,4,2,1,0:T(8,128)} fusion(f32[64,64,1,1]{1,0,3,2:T(8,128)S(1)} %bitcast.161, f32[64,2,64,64]{3,0,2,1:T(8,128)S(1)} %fusion.28), kind=kOutput, calls=%fused_computation.11 | convolution fusion | flops 402653184 | bytes 4210688 | tf_op jit(solution)/shard_map/gjc,gabcl->gabjl/dot_general | solution.py:129
  33.0 5.7 %copy.51 = f32[1,2,64,64,64]{4,3,2,1,0:T(8,128)} copy(f32[1,2,64,64,64]{3,4,2,1,0:T(8,128)} %fusion.4) | data formatting | bytes 4194304 | tf_op jit(solution)/shard_map/gjc,gabcl->gabjl/transpose | solution.py:129
  38.6 3.7 reshape.192
  43.0 0.2 fusion.12
  43.3 2.0 convolution_bitcast_fusion.2
  45.3 2.9 copy.52
  48.2 0.0 copy-start.2
  48.3 14.6 %all-to-all-start = ((f32[1,2,64,4096]{3,1,0,2:T(2,128)}), f32[1,2,64,4096]{3,1,0,2:T(2,128)S(1)}, u32[]{:S(2)}, u32[]{:S(2)}) async-start(f32[1,2,64,4096]{3,1,0,2:T(2,128)} %copy.52), calls=%async_computation | async-start | bytes 4194304 | tf_op jit(solution)/shard_map/all_to_all | solution.py:139
  62.8 0.0 all-reduce.2.cloned.1.call-start
  62.9 0.0 copy-done.3
  62.9 0.1 copy.50
  63.0 0.0 copy-done.4
  63.0 0.1 broadcast_add_fusion
  63.1 0.2 compare_reduce_fusion
  63.3 0.3 reduce_or.19
  63.6 0.0 copy-done.6
  63.7 0.1 select_reduce_fusion
  63.8 0.6 dynamic_slice.7
  64.4 0.0 copy-done.5
  64.4 0.1 broadcast_add_fusion.1
  64.5 0.1 and_reduce_fusion
  64.6 1.3 sort.17
  65.9 0.7 gather_fusion.1
  67.1 0.0 copy-done.2
  67.2 0.2 fusion.17
  67.4 45.5 %all-to-all-done = f32[1,2,64,4096]{3,1,0,2:T(2,128)S(1)} async-done(((f32[1,2,64,4096]{3,1,0,2:T(2,128)}), f32[1,2,64,4096]{3,1,0,2:T(2,128)S(1)}, u32[]{:S(2)}, u32[]{:S(2)}) %all-to-all-start) | async-done | bytes 2097184 | tf_op jit(solution)/shard_map/all_to_all | solution.py:139
  112.9 1.3 copy-done
  114.2 3.3 copy.53
  117.5 3.6 copy.54
  121.1 22.9 %multiply_bitcast_fusion = f32[4,2,2,16,2,32,32]{6,3,2,5,1,4,0:T(8,128)S(1)} fusion(f32[]{:T(128)} %bitcast.9, f32[4,16,64,1,1,1,1]{2,1,6,5,4,3,0:T(8,128)S(1)} %bitcast.157, f32[2,2,32,2,32,64,1]{5,4,3,2,1,0,6:T(8,128)} %bitcast.151), kind=kOutput, calls=%fused_computation.3 | convolution fusion | flops 403177472 | bytes 4210692 | tf_op jit(solution)/shard_map/gja,gabm->gjbm/dot_general | solution.py:136
  144.0 8.0 %copy.55 = f32[4,2,2,16,2,32,32]{6,5,4,3,2,1,0:T(8,128)} copy(f32[4,2,2,16,2,32,32]{6,3,2,5,1,4,0:T(8,128)S(1)} %multiply_bitcast_fusion) | data formatting | bytes 4194304 | tf_op jit(solution)/shard_map/transpose | solution.py:149
  152.0 6.1 %reshape.194 = f32[16,32768]{1,0:T(8,128)S(1)} reshape(f32[4,2,2,16,2,32,32]{6,5,4,3,2,1,0:T(8,128)} %copy.55) | data formatting | bytes 4194304 | tf_op jit(solution)/shard_map/reshape | solution.py:150
  158.1 2.4 gather_fusion
  160.5 3.1 select_multiply_fusion
  163.7 0.0 all-reduce.2.cloned.1.call-update
  163.7 0.9 copy-done.1
  164.6 0.2 fusion.18
  164.8 134.0 %all-reduce.2.cloned.1.call-done = f32[16,32768]{1,0:T(8,128)} async-done(((f32[16,32768]{1,0:T(8,128)}), f32[16,32768]{1,0:T(8,128)}) %all-reduce.2.cloned.1.call-update) | async-done | bytes 2097168 | tf_op jit(solution)/shard_map/psum | solution.py:102
  298.8 3.1 broadcast_multiply_fusion
  301.9 4.4 scatter_custom_fusion
  306.2 4.8 %reshape.195 = f32[4,2,2,16,2,32,32]{6,5,4,3,2,1,0:T(8,128)} reshape(f32[16,32768]{1,0:T(8,128)S(1)} %scatter_custom_fusion) | data formatting | bytes 4194304 | tf_op jit(solution)/shard_map/reshape | solution.py:154
  311.0 15.4 %copy.56 = f32[4,16,2,2,32,2,32]{6,5,4,3,1,0,2:T(2,128)} copy(f32[4,16,2,2,32,2,32]{6,4,2,1,5,3,0:T(8,128)} %bitcast.150) | data formatting | bytes 4194304 | tf_op jit(solution)/shard_map/transpose | solution.py:155
  326.4 12.2 %reshape.196 = f32[64,2,4096]{2,0,1:T(8,128)S(1)} reshape(f32[4,16,2,2,32,2,32]{6,5,4,3,1,0,2:T(2,128)} %copy.56) | data formatting | bytes 4194304 | tf_op jit(solution)/shard_map/reshape | solution.py:156
  338.6 1.9 convolution_bitcast_fusion.1
  340.5 2.9 copy.57
  343.4 20.4 %all-to-all-start.1 = ((f32[1,64,2,4096]{3,2,0,1:T(2,128)}), f32[1,64,2,4096]{3,2,0,1:T(2,128)S(1)}, u32[]{:S(2)}, u32[]{:S(2)}) async-start(f32[1,64,2,4096]{3,2,0,1:T(2,128)} %copy.57), calls=%async_computation.1 | async-start | bytes 4194304 | tf_op jit(solution)/shard_map/all_to_all | solution.py:159
  363.9 0.2 fusion.11
  364.1 0.2 fusion.13
  364.4 0.2 fusion.15
  364.6 49.2 %all-to-all-done.1 = f32[1,64,2,4096]{3,2,0,1:T(2,128)S(1)} async-done(((f32[1,64,2,4096]{3,2,0,1:T(2,128)}), f32[1,64,2,4096]{3,2,0,1:T(2,128)S(1)}, u32[]{:S(2)}, u32[]{:S(2)}) %all-to-all-start.1) | async-done | bytes 2097184 | tf_op jit(solution)/shard_map/all_to_all | solution.py:159
  413.8 1.5 copy.81
  415.2 3.7 reshape.197
  419.0 3.6 convolution_bitcast_fusion
  422.5 3.0 reshape.198
  425.5 8.6 %fusion.29 = f32[2,64,64,64]{3,2,1,0:T(8,128)S(1)} fusion(f32[2,64,64,64]{3,2,1,0:T(8,128)} %reshape.198, f32[64,64,1,1]{1,0,3,2:T(8,128)S(1)} %bitcast.159), kind=kOutput, calls=%fused_computation.66 | convolution fusion | flops 402653184 | bytes 4210688 | tf_op jit(solution)/shard_map/gjc,gabcl->gabjl/dot_general | solution.py:162
  434.2 8.4 %fusion = f32[2,64,64,64]{3,2,1,0:T(8,128)} fusion(f32[64,64,1,1]{1,0,3,2:T(8,128)S(1)} %bitcast.158, f32[2,64,64,64]{3,2,1,0:T(8,128)S(1)} %fusion.29), kind=kOutput, calls=%fused_computation.7 | convolution fusion | flops 402653184 | bytes 4210688 | tf_op jit(solution)/shard_map/gjl,gabcl->gabcj/dot_general | solution.py:163
  442.6 4.8 %reshape.200 = f32[1,2,64,4096]{3,2,1,0:T(8,128)} reshape(f32[2,64,64,64]{3,2,1,0:T(8,128)} %fusion) | data formatting | bytes 4194304 | tf_op jit(solution)/shard_map/reshape | solution.py:164
  (20 shorter events, 0.1 us)
Async XLA Ops:
  7.8 5.9 %copy-start.8 = (f32[2,64,64]{2,0,1:T(2,128)S(1)}, f32[2,64,64]{2,0,1:T(2,128)}, u32[]{:S(2)}) copy-start(f32[2,64,64]{2,0,1:T(2,128)} %constant.140) | copy-start | bytes 98308
  48.2 14.7 %copy-start.3 = (s32[16,4]{0,1:T(4,128)S(1)}, s32[16,4]{0,1:T(4,128)}, u32[]{:S(2)}) copy-start(s32[16,4]{0,1:T(4,128)} %param.14) | copy-start | bytes 772
  48.2 14.8 %copy-start.4 = (s32[16,4]{0,1:T(4,128)S(1)}, s32[16,4]{0,1:T(4,128)}, u32[]{:S(2)}) copy-start(s32[16,4]{0,1:T(4,128)} %constant.129.clone) | copy-start | bytes 772
  48.2 15.4 %copy-start.6 = (s32[16]{0:T(128)S(1)}, s32[16]{0:T(128)}, u32[]{:S(2)}) copy-start(s32[16]{0:T(128)} %constant.130.clone) | copy-start | bytes 196
  48.2 16.2 %copy-start.5 = (s32[4]{0:T(128)S(1)}, s32[4]{0:T(128)}, u32[]{:S(2)}) copy-start(s32[4]{0:T(128)} %constant.137) | copy-start | bytes 52
  48.2 18.9 %copy-start.2 = (f32[3,64,64]{2,0,1:T(4,128)S(1)}, f32[3,64,64]{2,0,1:T(4,128)}, u32[]{:S(2)}) copy-start(f32[3,64,64]{2,0,1:T(4,128)} %constant.139) | copy-start | bytes 147460
  48.3 64.7 %all-to-all-start = ((f32[1,2,64,4096]{3,1,0,2:T(2,128)}), f32[1,2,64,4096]{3,1,0,2:T(2,128)S(1)}, u32[]{:S(2)}, u32[]{:S(2)}) async-start(f32[1,2,64,4096]{3,1,0,2:T(2,128)} %copy.52), calls=%async_computation | async-start | bytes 4194304 | tf_op jit(solution)/shard_map/all_to_all | solution.py:139
  62.8 235.9 %all-reduce.2.cloned.1.call-start = ((), (), s32[]{:S(2)}) async-start(), calls=%async_computation.2 | async-start | bytes 4194304 | tf_op jit(solution)/shard_map/psum | solution.py:102
  112.9 1.3 copy-start
  163.6 0.9 copy-start.1
  343.4 20.4 %copy-start.7 = (f32[2,64,64]{2,0,1:T(2,128)S(1)}, f32[2,64,64]{2,0,1:T(2,128)}, u32[]{:S(2)}) copy-start(f32[2,64,64]{2,0,1:T(2,128)} %constant.141) | copy-start | bytes 98308
  343.4 70.3 %all-to-all-start.1 = ((f32[1,64,2,4096]{3,2,0,1:T(2,128)}), f32[1,64,2,4096]{3,2,0,1:T(2,128)S(1)}, u32[]{:S(2)}, u32[]{:S(2)}) async-start(f32[1,64,2,4096]{3,2,0,1:T(2,128)} %copy.57), calls=%async_computation.1 | async-start | bytes 4194304 | tf_op jit(solution)/shard_map/all_to_all | solution.py:159
Sparse Core Ops, SparseCore 0:
  163.8 134.9 all-reduce.1
where the time goes:
time: 461 us; the launch traced here: 455 us
  waiting for transfers between devices  229 us (50%)
  local copies, waits for them, and re-layouts  93.4 us (20%)
  matrix products  68.2 us (15%)
  starting transfers between devices  35 us (8%)
  between operations  16.5 us (4%)
  other arithmetic  12.8 us (3%)
    psum x1, waiting for transfers between devices, combine(): summed = lax.psum(pick_rows(blocks, order, valid), ('half', 'grid'))  134 us
    all_to_all x1, waiting for transfers between devices, per_device(): lax.all_to_all(expanded, 'dom', split_axis=1, concat_axis=2, tiled=True)  49.2 us
    all_to_all x1, waiting for transfers between devices, per_device(): lax.all_to_all(values, 'dom', split_axis=2, concat_axis=1, tiled=True)  45.5 us
    dot_general x1, matrix products, per_device(): jnp.einsum('gja,gabm->gjbm', forward_mats[0], lax.all_to_all(values, 'dom...  22.9 us
    all_to_all x1, starting transfers between devices, per_device(): lax.all_to_all(expanded, 'dom', split_axis=1, concat_axis=2, tiled=True)  20.4 us
    transpose x1, local copies, waits for them, and re-layouts, per_device(): totals = summed_blocks.reshape(4, 2, 2, quarter_rows, pole_rows, N3 // 2,...  15.4 us
    another operation x4, local copies, waits for them, and re-layouts  15.1 us
    all_to_all x1, starting transfers between devices, per_device(): lax.all_to_all(values, 'dom', split_axis=2, concat_axis=1, tiled=True)  14.6 us
  transfers between devices with their start and end apart: 3, of which 3 were waited for; matrix products, arithmetic and copies ran while one was open for 1% of the time, Pallas kernels for 0%

commit v1 on v0

--- a/solution.py
+++ b/solution.py
@@ -99,7 +99,7 @@
 
 def combine(blocks, covered):
     order, valid = compact_order(jnp.any(covered, axis=0))
-    summed = lax.psum(pick_rows(blocks, order, valid), ("half", "grid"))
+    summed = jnp.sum(lax.all_gather(pick_rows(blocks, order, valid), ("half", "grid")), axis=0)
     return place_rows(summed, order, valid)
 
 

time: 461 us -> 681 us (1.48)
  waiting for transfers between devices: 229 us -> 447 us
  other arithmetic: 12.8 us -> 23 us
  starting transfers between devices: 35 us -> 25.4 us
    all_gather x0 -> x1, waiting for transfers between devices: none -> 352 us  [combine(): lax.all_gather(pick_rows(blocks, order, valid), ('half', 'grid'))]
    psum x1 -> x0, waiting for transfers between devices: 134 us -> none  [combine(): summed = lax.psum(pick_rows(blocks, order, valid), ('half', 'grid'))]
    reduce_sum x0 -> x1, other arithmetic: none -> 11.7 us  [combine(): jnp.sum(lax.all_gather(pick_rows(blocks, order, valid), ('half', 'grid'))...]
    all_to_all x1, starting transfers between devices: 20.4 us -> 10.8 us  [per_device(): lax.all_to_all(expanded, 'dom', split_axis=1, concat_axis=2, tiled=True)]
where the time goes in v1:
time: 681 us; the launch traced here: 674 us
  waiting for transfers between devices  447 us (66%)
  local copies, waits for them, and re-layouts  93.4 us (14%)
  matrix products  68.2 us (10%)
  starting transfers between devices  25.4 us (4%)
  other arithmetic  23 us (3%)
  between operations  16.5 us (2%)
    all_gather x1, waiting for transfers between devices, combine(): lax.all_gather(pick_rows(blocks, order, valid), ('half', 'grid'))  352 us
    all_to_all x1, waiting for transfers between devices, per_device(): lax.all_to_all(expanded, 'dom', split_axis=1, concat_axis=2, tiled=True)  49.2 us
    all_to_all x1, waiting for transfers between devices, per_device(): lax.all_to_all(values, 'dom', split_axis=2, concat_axis=1, tiled=True)  45.5 us
    dot_general x1, matrix products, per_device(): jnp.einsum('gja,gabm->gjbm', forward_mats[0], lax.all_to_all(values, 'dom...  22.9 us
    transpose x1, local copies, waits for them, and re-layouts, per_device(): totals = summed_blocks.reshape(4, 2, 2, quarter_rows, pole_rows, N3 // 2,...  15.4 us
    another operation x4, local copies, waits for them, and re-layouts  15.1 us
    all_to_all x1, starting transfers between devices, per_device(): lax.all_to_all(values, 'dom', split_axis=2, concat_axis=1, tiled=True)  14.6 us
    dot_general x1, matrix products, per_device(): jnp.einsum('gjl,gabcl->gabcj', forward_mats[3], values, precision=HIGH)  13.8 us
  transfers between devices with their start and end apart: 3, of which 3 were waited for; matrix products, arithmetic and copies ran while one was open for 1% of the time, Pallas kernels for 0%

profile of v1, /device:TPU:1, one launch (start us, length us, event | category | flops | bytes accessed | tf_op | source)
XLA Modules:
  0.0 673.6 jit_solution(6602590551772174916)
XLA Ops:
  6.5 0.8 constant_dynamic-slice_fusion
  7.3 0.6 fusion.28
  7.8 4.6 reshape.237
  13.7 0.0 copy-done.8
  13.7 0.2 fusion.17
  14.0 0.2 fusion.15
  14.2 13.8 %fusion.29 = f32[64,2,64,64]{3,0,2,1:T(8,128)S(1)} fusion(f32[64,64,1,1]{1,0,3,2:T(8,128)S(1)} %bitcast.166, f32[2,64,64,64]{3,2,1,0:T(8,128)} %reshape.237), kind=kOutput, calls=%fused_computation.66 | convolution fusion | flops 402653184 | bytes 4210688 | tf_op jit(solution)/shard_map/gjl,gabcl->gabcj/dot_general | solution.py:128
  28.0 4.9 fusion.4
  33.0 5.7 copy.51
  38.6 3.7 reshape.238
  43.0 0.2 fusion.13
  43.3 2.0 convolution_bitcast_fusion.2
  45.3 2.9 copy.52
  48.2 0.0 copy-start.2
  48.3 14.6 %all-to-all-start = ((f32[1,2,64,4096]{3,1,0,2:T(2,128)}), f32[1,2,64,4096]{3,1,0,2:T(2,128)S(1)}, u32[]{:S(2)}, u32[]{:S(2)}) async-start(f32[1,2,64,4096]{3,1,0,2:T(2,128)} %copy.52), calls=%async_computation | async-start | bytes 4194304 | tf_op jit(solution)/shard_map/all_to_all | solution.py:139
  62.8 0.0 all-gather.2.cloned.1.call-start
  62.9 0.0 copy-done.3
  62.9 0.1 copy.50
  63.0 0.0 copy-done.4
  63.0 0.1 broadcast_add_fusion
  63.1 0.2 compare_reduce_fusion
  63.3 0.3 reduce_or.19
  63.6 0.0 copy-done.6
  63.7 0.1 select_reduce_fusion
  63.8 0.6 dynamic_slice.7
  64.4 0.0 copy-done.5
  64.4 0.1 broadcast_add_fusion.1
  64.5 0.1 and_reduce_fusion
  64.6 1.3 sort.17
  65.9 0.7 gather_fusion.1
  67.2 0.2 fusion.18
  67.4 45.5 %all-to-all-done = f32[1,2,64,4096]{3,1,0,2:T(2,128)S(1)} async-done(((f32[1,2,64,4096]{3,1,0,2:T(2,128)}), f32[1,2,64,4096]{3,1,0,2:T(2,128)S(1)}, u32[]{:S(2)}, u32[]{:S(2)}) %all-to-all-start) | async-done | bytes 2097184 | tf_op jit(solution)/shard_map/all_to_all | solution.py:139
  112.9 1.3 copy-done
  114.2 3.3 copy.53
  117.5 3.6 copy.54
  121.1 22.9 %multiply_bitcast_fusion = f32[4,2,2,16,2,32,32]{6,3,2,5,1,4,0:T(8,128)S(1)} fusion(f32[]{:T(128)} %bitcast.9, f32[4,16,64,1,1,1,1]{2,1,6,5,4,3,0:T(8,128)S(1)} %bitcast.161, f32[2,2,32,2,32,64,1]{5,4,3,2,1,0,6:T(8,128)} %bitcast.155), kind=kOutput, calls=%fused_computation.3 | convolution fusion | flops 403177472 | bytes 4210692 | tf_op jit(solution)/shard_map/gja,gabm->gjbm/dot_general | solution.py:136
  144.0 8.0 %copy.55 = f32[4,2,2,16,2,32,32]{6,5,4,3,2,1,0:T(8,128)} copy(f32[4,2,2,16,2,32,32]{6,3,2,5,1,4,0:T(8,128)S(1)} %multiply_bitcast_fusion) | data formatting | bytes 4194304 | tf_op jit(solution)/shard_map/transpose | solution.py:149
  152.0 6.1 reshape.240
  158.1 2.4 gather_fusion
  160.5 3.1 fusion.7
  163.7 0.0 all-gather.2.cloned.1.call-update
  163.7 0.9 copy-done.1
  164.6 0.2 fusion.19
  164.8 352.5 %all-gather.2.cloned.1.call-done = f32[16,16,32768]{2,1,0:T(8,128)} async-done(((f32[1,16,32768]{2,1,0:T(8,128)}), f32[16,16,32768]{2,1,0:T(8,128)}) %all-gather.2.cloned.1.call-update) | async-done | bytes 33554448 | tf_op jit(solution)/shard_map/all_gather | solution.py:102
  517.3 11.7 %reduce_sum.19 = f32[16,32768]{1,0:T(8,128)S(1)} reduce(f32[16,16,32768]{2,1,0:T(8,128)} %all-gather.2.cloned.1.call-done, f32[]{:T(128)} %constant.117.clone.1), dimensions={0}, to_apply=%region_5.6 | reduce | flops 7864320 | bytes 35651588 | tf_op jit(solution)/shard_map/reduce_sum | solution.py:102
  529.0 1.5 broadcast_multiply_fusion
  530.5 4.4 scatter_custom_fusion
  534.9 4.8 reshape.241
  539.7 15.4 %copy.56 = f32[4,16,2,2,32,2,32]{6,5,4,3,1,0,2:T(2,128)} copy(f32[4,16,2,2,32,2,32]{6,4,2,1,5,3,0:T(8,128)} %bitcast.154) | data formatting | bytes 4194304 | tf_op jit(solution)/shard_map/transpose | solution.py:155
  555.1 12.2 %reshape.242 = f32[64,2,4096]{2,0,1:T(8,128)S(1)} reshape(f32[4,16,2,2,32,2,32]{6,5,4,3,1,0,2:T(2,128)} %copy.56) | data formatting | bytes 4194304 | tf_op jit(solution)/shard_map/reshape | solution.py:156
  567.2 1.9 convolution_bitcast_fusion.1
  569.2 2.9 copy.57
  572.1 10.8 %all-to-all-start.1 = ((f32[1,64,2,4096]{3,2,0,1:T(2,128)}), f32[1,64,2,4096]{3,2,0,1:T(2,128)S(1)}, u32[]{:S(2)}, u32[]{:S(2)}) async-start(f32[1,64,2,4096]{3,2,0,1:T(2,128)} %copy.57), calls=%async_computation.1 | async-start | bytes 4194304 | tf_op jit(solution)/shard_map/all_to_all | solution.py:159
  582.9 0.2 fusion.12
  583.2 0.2 fusion.14
  583.4 0.2 fusion.16
  583.7 49.2 %all-to-all-done.1 = f32[1,64,2,4096]{3,2,0,1:T(2,128)S(1)} async-done(((f32[1,64,2,4096]{3,2,0,1:T(2,128)}), f32[1,64,2,4096]{3,2,0,1:T(2,128)S(1)}, u32[]{:S(2)}, u32[]{:S(2)}) %all-to-all-start.1) | async-done | bytes 2097184 | tf_op jit(solution)/shard_map/all_to_all | solution.py:159
  632.9 1.5 copy.81
  634.3 3.7 reshape.243
  638.0 3.6 convolution_bitcast_fusion
  641.6 3.0 reshape.244
  644.6 8.6 %fusion.30 = f32[2,64,64,64]{3,2,1,0:T(8,128)S(1)} fusion(f32[2,64,64,64]{3,2,1,0:T(8,128)} %reshape.244, f32[64,64,1,1]{1,0,3,2:T(8,128)S(1)} %bitcast.163), kind=kOutput, calls=%fused_computation.67 | convolution fusion | flops 402653184 | bytes 4210688 | tf_op jit(solution)/shard_map/gjc,gabcl->gabjl/dot_general | solution.py:162
  653.3 8.4 %fusion = f32[2,64,64,64]{3,2,1,0:T(8,128)} fusion(f32[64,64,1,1]{1,0,3,2:T(8,128)S(1)} %bitcast.162, f32[2,64,64,64]{3,2,1,0:T(8,128)S(1)} %fusion.30), kind=kOutput, calls=%fused_computation.7 | convolution fusion | flops 402653184 | bytes 4210688 | tf_op jit(solution)/shard_map/gjl,gabcl->gabcj/dot_general | solution.py:163
  661.6 4.8 reshape.246
  (21 shorter events, 0.1 us)
Async XLA Ops:
  7.8 5.9 copy-start.8
  48.2 14.7 %copy-start.3 = (s32[16,4]{0,1:T(4,128)S(1)}, s32[16,4]{0,1:T(4,128)}, u32[]{:S(2)}) copy-start(s32[16,4]{0,1:T(4,128)} %param.14) | copy-start | bytes 772
  48.2 14.8 %copy-start.4 = (s32[16,4]{0,1:T(4,128)S(1)}, s32[16,4]{0,1:T(4,128)}, u32[]{:S(2)}) copy-start(s32[16,4]{0,1:T(4,128)} %constant.130.clone) | copy-start | bytes 772
  48.2 15.4 %copy-start.6 = (s32[16]{0:T(128)S(1)}, s32[16]{0:T(128)}, u32[]{:S(2)}) copy-start(s32[16]{0:T(128)} %constant.131.clone) | copy-start | bytes 196
  48.2 16.2 %copy-start.5 = (s32[4]{0:T(128)S(1)}, s32[4]{0:T(128)}, u32[]{:S(2)}) copy-start(s32[4]{0:T(128)} %constant.138) | copy-start | bytes 52
  48.2 18.9 %copy-start.2 = (f32[3,64,64]{2,0,1:T(4,128)S(1)}, f32[3,64,64]{2,0,1:T(4,128)}, u32[]{:S(2)}) copy-start(f32[3,64,64]{2,0,1:T(4,128)} %constant.140) | copy-start | bytes 147460
  48.3 64.7 %all-to-all-start = ((f32[1,2,64,4096]{3,1,0,2:T(2,128)}), f32[1,2,64,4096]{3,1,0,2:T(2,128)S(1)}, u32[]{:S(2)}, u32[]{:S(2)}) async-start(f32[1,2,64,4096]{3,1,0,2:T(2,128)} %copy.52), calls=%async_computation | async-start | bytes 4194304 | tf_op jit(solution)/shard_map/all_to_all | solution.py:139
  62.8 454.5 %all-gather.2.cloned.1.call-start = ((), (), s32[]{:S(2)}) async-start(), calls=%async_computation.2 | async-start | bytes 35651584 | tf_op jit(solution)/shard_map/all_gather | solution.py:102
  112.9 1.3 copy-start
  163.6 0.9 copy-start.1
  572.1 10.8 %copy-start.7 = (f32[2,64,64]{2,0,1:T(2,128)S(1)}, f32[2,64,64]{2,0,1:T(2,128)}, u32[]{:S(2)}) copy-start(f32[2,64,64]{2,0,1:T(2,128)} %constant.142) | copy-start | bytes 98308
  572.1 60.7 %all-to-all-start.1 = ((f32[1,64,2,4096]{3,2,0,1:T(2,128)}), f32[1,64,2,4096]{3,2,0,1:T(2,128)S(1)}, u32[]{:S(2)}, u32[]{:S(2)}) async-start(f32[1,64,2,4096]{3,2,0,1:T(2,128)} %copy.57), calls=%async_computation.1 | async-start | bytes 4194304 | tf_op jit(solution)/shard_map/all_to_all | solution.py:159
Sparse Core Ops, SparseCore 0:
  163.8 353.4 all-gather.1
